TPU v7x, 32 devices: a whole 2x2x4 slice. The times are simulated.
32 devices in a mesh: groups: 2 (over y), wide: 4 (over z), node: 4 (over x, core).
Axes of the slice: x: 2, y: 2, z: 4, core: 2. Of those that a mesh axis runs over, the one named last changes fastest.
Arguments:
- tokens: bfloat16 [1024, 2304], P(('groups', 'wide')), parts along dimension 0, may hold values from -6 to 6
- cotangent: bfloat16 [1024, 2304], P(('groups', 'wide')), parts along dimension 0, may hold values from -1.5 to 1.5
- tiles: bfloat16 [4, 4, 25, 128, 128], P('node', 'wide'), may hold values from -0.125 to 0.125
- tile_ids: int32 [4, 4, 25], P('node', 'wide'), may hold values from 0 to 215, as said below
- tile_counts: int32 [4, 4], P('node', 'wide'), may hold values from 0 to 25, as said below
Outputs:
- mixed: bfloat16 [1024, 2304], P(('groups', 'wide')), parts along dimension 0
- input_grad: bfloat16 [1024, 2304], P(('groups', 'wide')), parts along dimension 0
- grad_tiles: bfloat16 [8, 4, 25, 128, 128], P(('groups', 'node'), 'wide'), parts along dimension 0
There are 2 independent parts, one for each index of `groups`. A program takes and returns all parts, laid end to end along the dimension named above; an argument that names none is the same for every part. Nothing has to cross between parts.
Inputs may be any that keep to these rules, and one draw needn't show every extreme that they name: `tile_ids`: for each index of node, the live slots of all indices of wide name 97 different blocks; slots that are not live hold any block number. `tile_counts`: for each index of node the counts sum to 97.
All inputs are finite; a program needn't handle non-finite values.
Results may differ from a plain program's by a relative error of at most 0.0095.
Values may be sent and summed in bfloat16 or wider, within the bound.
A program may use at most 64 MiB of HBM per device.

v0:
```python
import math

import jax
import jax.numpy as jnp
from jax import lax
from jax.sharding import PartitionSpec as P

FF_DEV = 512
NBLK = 216


gelu_scale = math.sqrt(2.0 / math.pi)
cubic_term = 0.044715


def gelu_parts(pre):
    tangent = jnp.tanh(gelu_scale * (pre + cubic_term * pre * pre * pre))
    value = 0.5 * pre * (1.0 + tangent)
    slope = 0.5 * (1.0 + tangent) + 0.5 * pre * (1.0 - tangent * tangent) * gelu_scale * (
        1.0 + 3.0 * cubic_term * pre * pre
    )
    return (value, slope)


def contract_rows(left, right):
    return lax.dot_general(
        left, right, (((1,), (1,)), ((), ())), preferred_element_type=jnp.float32
    )


def contract_tokens(left, right):
    return lax.dot_general(
        left, right, (((0,), (0,)), ((), ())), preferred_element_type=jnp.float32
    )


def select_slots(block_ids, counts):
    slot_count = block_ids.shape[2]
    slot_index = jnp.arange(slot_count, dtype=jnp.int32)
    live_slots = (slot_index[None, None, :] < counts[:, :, None]).reshape(-1)
    numbers = jnp.arange(NBLK, dtype=jnp.int32)
    matches = (block_ids.reshape(-1)[None, :] == numbers[:, None]) & live_slots[None, :]
    return matches.astype(jnp.bfloat16)


def place_blocks(onehot, slot_tiles):
    edge = slot_tiles.shape[-1]
    flat_rows = slot_tiles.reshape(-1, edge * edge)
    return jnp.dot(onehot, flat_rows, preferred_element_type=jnp.float32)


def to_dense(flat_rows, width, edge):
    shaped = flat_rows.reshape(3, width // edge, FF_DEV // edge, edge, edge)
    return shaped.transpose(0, 1, 3, 2, 4).reshape(3, width, FF_DEV)


def block_rows(dense, width, edge):
    shaped = dense.reshape(3, width // edge, edge, FF_DEV // edge, edge)
    return shaped.transpose(0, 1, 3, 2, 4).reshape(NBLK, edge * edge)


def per_device(tokens, cotangent, tiles, tile_ids, tile_counts):
    edge = tiles.shape[-1]
    slot_count = tiles.shape[2]
    width = tokens.shape[1]
    wide_count = lax.axis_size("wide")
    gathered = (
        lax.all_gather(tiles, "wide", axis=1, tiled=True),
        lax.all_gather(tile_ids, "wide", axis=1, tiled=True),
        lax.all_gather(tile_counts, "wide", axis=1, tiled=True),
    )
    onehot = select_slots(gathered[1], gathered[2])
    placed = place_blocks(onehot, gathered[0]).astype(jnp.bfloat16)
    weights = to_dense(placed, width, edge)
    gate_pre = jnp.dot(tokens, weights[0], preferred_element_type=jnp.float32)
    up_pre = jnp.dot(tokens, weights[1], preferred_element_type=jnp.float32)
    value, slope = gelu_parts(gate_pre)
    hidden = (value * up_pre).astype(jnp.bfloat16)
    out_part = contract_rows(hidden, weights[2])
    mixed = lax.psum(out_part.astype(jnp.bfloat16), "node")
    again = (
        lax.all_gather(tiles, "wide", axis=1, tiled=True),
        lax.all_gather(tile_ids, "wide", axis=1, tiled=True),
        lax.all_gather(tile_counts, "wide", axis=1, tiled=True),
    )
    onehot = select_slots(again[1], again[2])
    weights = to_dense(place_blocks(onehot, again[0]).astype(jnp.bfloat16), width, edge)
    hidden_grad = jnp.dot(cotangent, weights[2], preferred_element_type=jnp.float32)
    gate_grad = (hidden_grad * up_pre * slope).astype(jnp.bfloat16)
    up_grad = (hidden_grad * value).astype(jnp.bfloat16)
    input_part = contract_rows(gate_grad, weights[0]) + contract_rows(up_grad, weights[1])
    input_grad = lax.psum(input_part.astype(jnp.bfloat16), "node")
    dense_grads = jnp.stack(
        [
            contract_tokens(tokens, gate_grad).astype(jnp.bfloat16),
            contract_tokens(tokens, up_grad).astype(jnp.bfloat16),
            contract_tokens(cotangent, hidden).astype(jnp.bfloat16),
        ]
    )
    slot_terms = lax.dot_general(
        onehot,
        block_rows(dense_grads, width, edge),
        (((0,), (0,)), ((), ())),
        preferred_element_type=jnp.float32,
    )
    slot_terms = slot_terms.reshape(1, wide_count, slot_count, edge, edge)
    grad_tiles = lax.psum_scatter(
        slot_terms.astype(jnp.bfloat16), "wide", scatter_dimension=1, tiled=True
    )
    return (mixed, input_grad, grad_tiles)


def solution(mesh):
    return jax.shard_map(
        per_device,
        mesh=mesh,
        in_specs=(
            P(("groups", "wide"), None),
            P(("groups", "wide"), None),
            P("node", "wide", None, None, None),
            P("node", "wide", None),
            P("node", "wide"),
        ),
        out_specs=(
            P(("groups", "wide"), None),
            P(("groups", "wide"), None),
            P(("groups", "node"), "wide", None, None, None),
        ),
        check_vma=False,
    )
```

profile of v0, /device:TPU:1, one launch (start us, length us, event | category | flops | bytes accessed | tf_op | source)
XLA Modules:
  0.0 301.6 jit_solution(9856029168344432173)
XLA Ops:
  7.2 0.0 all-gather.2.cloned.1.call-start
  7.2 0.7 all-gather.2.cloned.1.call-update
  7.9 0.0 reduce-scatter.2.cloned.1.call-start
  8.6 1.2 dynamic-slice
  9.9 0.7 bitcast_dynamic-update-slice_fusion
  10.5 7.3 %all-reduce = s32[4]{0:T(128)S(1)} all-reduce(s32[4]{0:T(128)S(1)} %bitcast_dynamic-update-slice_fusion), channel_id=1, replica_groups=mesh['groups'=2,'wide'=4,'node'=4] {'wide'}, use_global_device_ids=true, to_apply=%add | all-reduce | flops 4 | bytes 32 | tf_op jit(solution)/shard_map/all_gather | solution.py:70
  17.8 0.1 lt.39
  17.9 0.1 lt.40
  18.0 7.3 %all_gather.14 = s32[1,4,25]{2,0,1:T(1,128)S(1)} all-gather(s32[1,1,25]{2,0,1:T(1,128)} %bitcast.120), channel_id=1, replica_groups=mesh['groups'=2,'wide'=4,'node'=4] {'wide'}, dimensions={1}, use_global_device_ids=true | all-gather | bytes 500 | tf_op jit(solution)/shard_map/all_gather | solution.py:69
  25.3 0.5 broadcast.71
  25.8 0.7 reduce.3
  26.5 0.1 eq.41
  26.6 0.1 lt.38
  26.7 0.1 iota_compare_fusion.2
  26.8 50.6 %all-gather.2.cloned.1.call-done = bf16[1,4,25,128,128]{4,3,2,0,1:T(8,128)(2,1)} async-done(((bf16[1,1,25,128,128]{4,3,2,0,1:T(8,128)(2,1)}), bf16[1,4,25,128,128]{4,3,2,0,1:T(8,128)(2,1)}) %all-gather.2.cloned.1.call-update) | async-done | bytes 3276816 | tf_op jit(solution)/shard_map/all_gather | solution.py:68
  77.3 2.2 pad.3
  79.6 2.7 copy.27
  82.3 2.0 fusion.2
  84.3 5.0 %copy.28 = bf16[27,8,128,128]{3,2,1,0:T(8,128)(2,1)} copy(bf16[27,8,128,128]{3,1,2,0:T(8,128)(2,1)S(1)} %fusion.2) | data formatting | bytes 14155776
  89.4 16.5 %copy.75 = bf16[3,18,4,128,128]{4,2,3,1,0:T(4,128)(2,1)} copy(bf16[3,18,4,128,128]{4,3,2,1,0:T(8,128)(2,1)} %bitcast.107) | data formatting | bytes 14155776 | tf_op jit(solution)/shard_map/reshape | solution.py:53
  105.9 4.6 %fusion.48 = (bf16[1,18,128,4,128]{4,3,2,1,0:T(4,128)(2,1)S(1)}, bf16[1,18,128,4,128]{4,3,2,1,0:T(4,128)(2,1)S(1)}, bf16[1,18,128,4,128]{4,3,2,1,0:T(4,128)(2,1)S(1)}) fusion(bf16[3,18,128,4,128]{4,3,2,1,0:T(4,128)(2,1)} %bitcast.106), kind=kLoop, calls=%fused_computation.60 | loop fusion | bytes 14155776 | tf_op jit(solution)/shard_map/slice | solution.py:79
  110.6 0.8 fusion.26
  111.4 0.9 fusion.23
  112.3 0.4 copy-done.4
  112.7 0.2 copy-done.5
  112.9 1.6 multiply_convert_fusion
  114.5 0.7 copy-done.6
  115.1 2.2 fusion.4
  117.3 4.3 %copy.20 = bf16[2304,512]{1,0:T(8,128)(2,1)} copy(bf16[2304,512]{0,1:T(8,128)(2,1)} %fusion.4) | data formatting | bytes 4718592 | tf_op jit(solution)/shard_map/convert_element_type | solution.py:96
  121.6 5.3 %stack.13 = bf16[1,18,128,4,128]{4,3,2,1,0:T(4,128)(2,1)} reshape(bf16[2304,512]{1,0:T(8,128)(2,1)} %copy.20) | data formatting | bytes 4718592 | tf_op jit(solution)/shard_map/stack | solution.py:93
  126.9 3.1 %fusion.3 = bf16[2304,512]{0,1:T(8,128)(2,1)} fusion(bf16[128,512]{0,1:T(8,128)(2,1)} %get-tuple-element.18, bf16[128,2304]{1,0:T(8,128)(2,1)S(1)} %copy-done), kind=kOutput, calls=%fused_computation.12 | convolution fusion | flops 303169536 | bytes 3080192 | tf_op jit(solution)/shard_map/dot_general | solution.py:32
  129.9 4.3 %copy.19 = bf16[2304,512]{1,0:T(8,128)(2,1)} copy(bf16[2304,512]{0,1:T(8,128)(2,1)} %fusion.3) | data formatting | bytes 4718592 | tf_op jit(solution)/shard_map/convert_element_type | solution.py:95
  134.2 5.3 %stack.12 = bf16[1,18,128,4,128]{4,3,2,1,0:T(4,128)(2,1)} reshape(bf16[2304,512]{1,0:T(8,128)(2,1)} %copy.19) | data formatting | bytes 4718592 | tf_op jit(solution)/shard_map/stack | solution.py:93
  139.6 2.2 fusion.5
  141.8 4.4 %copy.21 = bf16[2304,512]{1,0:T(8,128)(2,1)} copy(bf16[2304,512]{0,1:T(8,128)(2,1)} %fusion.5) | data formatting | bytes 4718592 | tf_op jit(solution)/shard_map/convert_element_type | solution.py:97
  146.1 5.3 %stack.14 = bf16[1,18,128,4,128]{4,3,2,1,0:T(4,128)(2,1)} reshape(bf16[2304,512]{1,0:T(8,128)(2,1)} %copy.21) | data formatting | bytes 4718592 | tf_op jit(solution)/shard_map/stack | solution.py:93
  151.4 8.0 %maximum_bitcast_fusion = bf16[3,18,4,128,128]{4,2,3,1,0:T(4,128)(2,1)S(1)} fusion(bf16[1,18,128,4,128]{4,3,2,1,0:T(4,128)(2,1)} %stack.14, bf16[1,18,128,4,128]{4,3,2,1,0:T(4,128)(2,1)} %stack.13, bf16[1,18,128,4,128]{4,3,2,1,0:T(4,128)(2,1)} %stack.12), kind=kLoop, calls=%fused_computation.5 | loop fusion | flops 7077888 | bytes 14155776 | tf_op jit(solution)/shard_map/transpose | solution.py:59
  159.5 4.9 %copy.22 = bf16[3,18,4,128,128]{4,3,2,1,0:T(8,128)(2,1)} copy(bf16[3,18,4,128,128]{4,2,3,1,0:T(4,128)(2,1)S(1)} %maximum_bitcast_fusion) | data formatting | bytes 14155776 | tf_op jit(solution)/shard_map/transpose | solution.py:59
  164.4 10.2 %convert_bitcast_fusion = bf16[1,4,25,128,128]{4,2,3,1,0:T(8,128)(2,1)} fusion(s32[4,25]{1,0:T(4,128)S(1)} %bitcast.119, pred[4,25]{1,0:T(4,128)(4,1)S(1)} %iota_compare_fusion.2, bf16[27,8,128,128]{3,2,1,0:T(8,128)(2,1)} %bitcast.114), kind=kOutput, calls=%fused_computation.11 | convolution fusion | flops 709470400 | bytes 10355188 | tf_op jit(solution)/shard_map/dot_general | solution.py:100
  174.6 0.0 all-reduce.4.cloned.1.call-start
  174.7 3.5 %convolution_convert_fusion.4 = bf16[128,2304]{1,0:T(8,128)(2,1)} fusion(bf16[128,512]{0,1:T(8,128)(2,1)S(1)} %copy-done.9, bf16[288,8,4,128]{3,2,1,0:T(4,128)(2,1)} %bitcast.117), kind=kOutput, calls=%fused_computation.17 | convolution fusion | flops 302284800 | bytes 3080192 | tf_op jit(solution)/shard_map/dot_general | solution.py:26
  178.3 0.9 fusion.13
  179.2 1.8 fusion.6
  181.0 69.3 %reduce-scatter.2.cloned.1.call-done = bf16[1,1,25,128,128]{4,2,3,1,0:T(8,128)(2,1)} async-done(((bf16[1,4,25,128,128]{4,2,3,1,0:T(8,128)(2,1)}), bf16[1,1,25,128,128]{4,2,3,1,0:T(8,128)(2,1)}) %reduce-scatter.2.cloned.1.call-update) | async-done | bytes 819216 | tf_op jit(solution)/shard_map/reduce_scatter | solution.py:107
  250.3 2.4 copy.24
  252.7 38.6 %all-reduce.4.cloned.1.call-done = (bf16[128,2304]{1,0:T(8,128)(2,1)}, bf16[128,2304]{1,0:T(8,128)(2,1)}) async-done(((bf16[128,2304]{1,0:T(8,128)(2,1)}, bf16[128,2304]{1,0:T(8,128)(2,1)}), (bf16[128,2304]{1,0:T(8,128)(2,1)}, bf16[128,2304]{1,0:T(8,128)(2,1)})) %all-reduce.4.cloned.1.call-update) | async-done | bytes 1179664 | tf_op jit(solution)/shard_map/psum | solution.py:80
  291.3 1.9 copy.80
  293.2 1.9 copy.81
  (22 shorter events, 0.1 us)
Async XLA Ops:
  7.2 103.4 %copy-start = (bf16[128,2304]{1,0:T(8,128)(2,1)S(1)}, bf16[128,2304]{1,0:T(8,128)(2,1)}, u32[]{:S(2)}) copy-start(bf16[128,2304]{1,0:T(8,128)(2,1)} %param.5) | copy-start | bytes 1769476
  7.2 70.2 %all-gather.2.cloned.1.call-start = ((), (), s32[]{:S(2)}) async-start(), calls=%async_computation.1 | async-start | bytes 4096000 | tf_op jit(solution)/shard_map/all_gather | solution.py:68
  7.9 242.4 %reduce-scatter.2.cloned.1.call-start = ((), (), s32[]{:S(2)}) async-start(), calls=%async_computation.2 | async-start | bytes 5242880 | tf_op jit(solution)/shard_map/reduce_scatter | solution.py:107
  110.5 1.7 copy-start.2
  110.5 2.2 copy-start.4
  111.4 1.5 copy-start.5
  114.5 0.7 copy-start.6
  134.2 5.3 %copy-start.9 = (bf16[128,512]{0,1:T(8,128)(2,1)S(1)}, bf16[128,512]{0,1:T(8,128)(2,1)}, u32[]{:S(2)}) copy-start(bf16[128,512]{0,1:T(8,128)(2,1)} %get-tuple-element.19) | copy-start | bytes 393220
  174.6 3.6 %copy-start.8 = (bf16[128,512]{0,1:T(8,128)(2,1)S(1)}, bf16[128,512]{0,1:T(8,128)(2,1)}, u32[]{:S(2)}) copy-start(bf16[128,512]{0,1:T(8,128)(2,1)} %get-tuple-element.18) | copy-start | bytes 393220
  174.6 116.6 %all-reduce.4.cloned.1.call-start = ((), (), s32[]{:S(2)}) async-start(), calls=%async_computation.3 | async-start | bytes 2359296 | tf_op jit(solution)/shard_map/psum | solution.py:80
  174.7 3.6 %copy-start.3 = (bf16[1,18,128,4,128]{4,3,2,1,0:T(4,128)(2,1)S(1)}, bf16[1,18,128,4,128]{4,3,2,1,0:T(4,128)(2,1)}, u32[]{:S(2)}) copy-start(bf16[1,18,128,4,128]{4,3,2,1,0:T(4,128)(2,1)} %copy-done.2) | copy-start | bytes 7077892
  178.3 0.9 copy-start.7
  181.0 114.1 %copy-start.1 = (bf16[128,2304]{1,0:T(8,128)(2,1)S(1)}, bf16[128,2304]{1,0:T(8,128)(2,1)}, u32[]{:S(2)}) copy-start(bf16[128,2304]{1,0:T(8,128)(2,1)} %param.5) | copy-start | bytes 1769476
Sparse Core Ops, SparseCore 0:
  9.6 67.7 all-gather.1
  174.8 75.4 reduce-scatter.1
  253.4 37.8 all-reduce.3
where the time goes:
time: 303 us; the launch traced here: 302 us
  waiting for transfers between devices  159 us (52%)
  local copies, waits for them, and re-layouts  75.2 us (25%)
  matrix products  29.2 us (10%)
  blocking collectives  14.6 us (5%)
  between operations  14.5 us (5%)
  other arithmetic  8.77 us (3%)
    reduce_scatter x1, waiting for transfers between devices, per_device(): lax.psum_scatter(slot_terms.astype(jnp.bfloat16), 'wide', scatter_dimensi...  69.3 us
    all_gather x1, waiting for transfers between devices, per_device(): lax.all_gather(tiles, 'wide', axis=1, tiled=True)  50.6 us
    psum x1, waiting for transfers between devices, per_device(): mixed = lax.psum(out_part.astype(jnp.bfloat16), 'node')  38.6 us
    unnamed x29, local copies, waits for them, and re-layouts  19.5 us
    reshape x1, local copies, waits for them, and re-layouts, to_dense(): shaped = flat_rows.reshape(3, width // edge, FF_DEV // edge, edge, edge)  16.5 us
    another operation x3, local copies, waits for them, and re-layouts, per_device(): jnp.stack([contract_tokens(tokens, gate_grad).astype(jnp.bfloat16), contr...  15.9 us
    dot_general x1, matrix products, per_device(): lax.dot_general(onehot, block_rows(dense_grads, width, edge), (((0,), (0,...  10.2 us
    transpose x1, other arithmetic, block_rows(): return shaped.transpose(0, 1, 3, 2, 4).reshape(NBLK, edge * edge)  8.02 us
  transfers between devices with their start and end apart: 3, of which 3 were waited for; matrix products, arithmetic and copies ran while one was open for 4% of the time, Pallas kernels for 0%

commit v1 on v0

v1 whole, which is shorter than its diff:
```python
import functools
import math

import jax
import jax.numpy as jnp
from jax import lax
from jax.experimental import pallas as pl
from jax.experimental.pallas import tpu as pltpu
from jax.sharding import PartitionSpec as P

FF_DEV = 512
NBLK = 216
EDGE = 128
COLS = FF_DEV // EDGE
MESH = pl.DeviceIdType.MESH

gelu_scale = math.sqrt(2.0 / math.pi)
cubic_term = 0.044715


def gelu_parts(pre):
    tangent = jnp.tanh(gelu_scale * (pre + cubic_term * pre * pre * pre))
    value = 0.5 * pre * (1.0 + tangent)
    slope = 0.5 * (1.0 + tangent) + 0.5 * pre * (1.0 - tangent * tangent) * gelu_scale * (
        1.0 + 3.0 * cubic_term * pre * pre
    )
    return (value, slope)


def contract_rows(left, right):
    return lax.dot_general(
        left, right, (((1,), (1,)), ((), ())), preferred_element_type=jnp.float32
    )


def contract_tokens(left, right):
    return lax.dot_general(
        left, right, (((0,), (0,)), ((), ())), preferred_element_type=jnp.float32
    )


def remote(src, dst, send, recv, where):
    return pltpu.make_async_remote_copy(
        src_ref=src, dst_ref=dst, send_sem=send, recv_sem=recv, device_id=where, device_id_type=MESH
    )


def gather_kernel(n_wide, chunks, tiles_ref, ids_ref, all_ref, allids_ref,
                  zsend, zrecv, ysend, yrecv, isend, irecv, own_sem):
    w = lax.axis_index("wide")
    g = lax.axis_index("groups")
    other = 1 - g
    rows = tiles_ref.shape[0]
    half = rows // 2
    step = half // chunks

    barrier = pltpu.get_barrier_semaphore()
    for d in range(1, n_wide):
        pl.semaphore_signal(barrier, inc=1, device_id={"wide": lax.rem(w + d, n_wide)}, device_id_type=MESH)
    pl.semaphore_signal(barrier, inc=1, device_id={"groups": other}, device_id_type=MESH)
    own = pltpu.make_async_copy(tiles_ref, all_ref.at[pl.ds(pl.multiple_of(w * rows, 16), rows)], own_sem)
    own.start()
    all_ref[n_wide * rows:, :] = jnp.zeros((EDGE, EDGE), all_ref.dtype)
    allids_ref[w] = ids_ref[...]
    pl.semaphore_wait(barrier, n_wide)

    def part(group, k):
        return pl.ds(pl.multiple_of(group * half + k * step, 16), step)

    def piece(j, group, k):
        return all_ref.at[pl.ds(pl.multiple_of(j * rows + group * half + k * step, 16), step)]

    def z_copy(j, k, way):
        return remote(
            piece(j, g, k), piece(j, g, k),
            zsend.at[0 if way > 0 else 1, j, k], zrecv.at[j, k], {"wide": w + way},
        )

    def z_own(k, way):
        return remote(
            tiles_ref.at[part(g, k)], piece(w, g, k),
            zsend.at[0 if way > 0 else 1, w, k], zrecv.at[w, k], {"wide": w + way},
        )

    def y_copy(j, k, group):
        return remote(
            piece(j, group, k), piece(j, group, k),
            ysend.at[j, k], yrecv.at[j, k], {"groups": other},
        )

    def ids_copy(d):
        to = lax.rem(w + d, n_wide)
        return remote(allids_ref.at[w], allids_ref.at[w], isend.at[d], irecv.at[w], {"wide": to})

    right = w < n_wide - 1
    left = w > 0
    for k in range(chunks):
        @pl.when(right)
        def _():
            z_own(k, 1).start()

        @pl.when(left)
        def _():
            z_own(k, -1).start()
    for d in range(1, n_wide):
        ids_copy(d).start()
    for d in range(1, n_wide):
        for k in range(chunks):
            for way in (1, -1):
                j = w - d * way
                have = (j >= 0) if way > 0 else (j < n_wide)

                @pl.when(have)
                def _():
                    z_copy(j, k, way).wait_recv()

                @pl.when(have & (right if way > 0 else left))
                def _():
                    z_copy(j, k, way).start()

                @pl.when(have)
                def _():
                    y_copy(j, k, g).start()
    own.wait()
    for k in range(chunks):
        @pl.when(right)
        def _():
            z_own(k, 1).wait_send()

        @pl.when(left)
        def _():
            z_own(k, -1).wait_send()
    for d in range(1, n_wide):
        ids_copy(d).wait_send()
        j = lax.rem(w + d, n_wide)
        remote(allids_ref.at[j], allids_ref.at[j], isend.at[d], irecv.at[j], {"wide": j}).wait_recv()
        for k in range(chunks):
            y_copy(j, k, g).wait_send()
            y_copy(j, k, other).wait_recv()
            for way in (1, -1):
                i = w - d * way
                have = (i >= 0) if way > 0 else (i < n_wide)

                @pl.when(have & (right if way > 0 else left))
                def _():
                    z_copy(i, k, way).wait_send()


def gather_tiles(tiles, ids, n_wide):
    rows = tiles.shape[0]
    chunks = 5 if (rows // 2) % 80 == 0 else 1
    dma = pltpu.SemaphoreType.DMA
    vmem = pl.BlockSpec(memory_space=pltpu.VMEM)
    return pl.pallas_call(
        functools.partial(gather_kernel, n_wide, chunks),
        out_shape=(
            jax.ShapeDtypeStruct((n_wide * rows + EDGE, EDGE), tiles.dtype),
            jax.ShapeDtypeStruct((n_wide,) + ids.shape, ids.dtype),
        ),
        in_specs=[vmem, vmem],
        out_specs=(vmem, vmem),
        scratch_shapes=[
            dma((2, n_wide, chunks)), dma((n_wide, chunks)), dma((n_wide, chunks)), dma((n_wide, chunks)),
            dma((n_wide,)), dma((n_wide,)), dma,
        ],
        compiler_params=pltpu.CompilerParams(
            collective_id=0, has_side_effects=True, vmem_limit_bytes=40 << 20
        ),
    )(tiles, ids)


def main_kernel(n_wide, n_node,
                inv_ref, tok_ref, cot_ref, tiles_ref,
                mixed_ref, input_ref, gath_ref, acts_ref,
                weights, acts, parts, arrived,
                xsend, xrecv, nsend, nrecv, hsend, hrecv, psend, precv, osend, orecv, ssem):
    w = lax.axis_index("wide")
    n = lax.axis_index("node")
    toks, width = tok_ref.shape
    piece = toks // n_node
    rblocks = width // EDGE
    per = rblocks * COLS
    bits = n_node.bit_length() - 1

    barrier = pltpu.get_barrier_semaphore()
    for d in range(1, n_wide):
        pl.semaphore_signal(barrier, inc=1, device_id={"wide": lax.rem(w + d, n_wide)}, device_id_type=MESH)
    for d in range(1, n_node):
        pl.semaphore_signal(barrier, inc=1, device_id={"node": lax.rem(n + d, n_node)}, device_id_type=MESH)

    def rows_of(j, q):
        return pl.ds(pl.multiple_of(j * toks + q * piece, 16), piece)

    own_rows = pl.ds(pl.multiple_of(w * toks, 16), toks)
    def keep(t):
        return pltpu.make_async_copy((tok_ref, cot_ref)[t], gath_ref.at[t, own_rows, :], ssem.at[t])

    keep(0).start()
    keep(1).start()
    pl.semaphore_wait(barrier, n_wide + n_node - 2)

    def x_copy(j, d, t):
        mine = (tok_ref, cot_ref)[t].at[pl.ds(pl.multiple_of(n * piece, 16), piece), :]
        return remote(
            mine, gath_ref.at[t, rows_of(j, n), :], xsend.at[d, t], xrecv.at[j, t],
            {"wide": lax.rem(w + d, n_wide)},
        )

    for d in range(1, n_wide):
        for t in range(2):
            x_copy(w, d, t).start()

    def place(r, _):
        for m in range(3):
            for c in range(COLS):
                i = inv_ref[m * per + r * COLS + c]
                weights[m, pl.ds(pl.multiple_of(r * EDGE, EDGE), EDGE), c * EDGE:(c + 1) * EDGE] = tiles_ref[i]
        return 0

    lax.fori_loop(0, rblocks, place, 0)

    gate = jnp.dot(tok_ref[...], weights[0], preferred_element_type=jnp.float32)
    up = jnp.dot(tok_ref[...], weights[1], preferred_element_type=jnp.float32)
    value, slope = gelu_parts(gate)
    hidden = (value * up).astype(jnp.bfloat16)
    hidden_grad = jnp.dot(cot_ref[...], weights[2], preferred_element_type=jnp.float32)
    gate_grad = (hidden_grad * up * slope).astype(jnp.bfloat16)
    up_grad = (hidden_grad * value).astype(jnp.bfloat16)
    acts[0] = gate_grad
    acts[1] = up_grad
    acts[2] = hidden
    keep_acts = pltpu.make_async_copy(acts, acts_ref.at[:, own_rows, :], ssem.at[2])
    keep_acts.start()

    def h_copy(j, d):
        at = acts_ref.at[:, pl.ds(pl.multiple_of(j * toks, 16), toks), :]
        return remote(acts, at, hsend.at[d], hrecv.at[j], {"wide": lax.rem(w + d, n_wide)})

    for d in range(1, n_wide):
        h_copy(w, d).start()

    def p_copy(t, src, to, d):
        return remote(
            parts.at[t, pl.ds(pl.multiple_of(to * piece, 16), piece), :], arrived.at[t, src],
            psend.at[t, d], precv.at[t, src], {"node": to},
        )

    out_part = contract_rows(hidden, weights[2])
    parts[0] = out_part.astype(jnp.bfloat16)
    for d in range(1, n_node):
        p_copy(0, n, lax.rem(n + d, n_node), d).start()
    parts[1] = (contract_rows(gate_grad, weights[0]) + contract_rows(up_grad, weights[1])).astype(jnp.bfloat16)
    for d in range(1, n_node):
        p_copy(1, n, lax.rem(n + d, n_node), d).start()

    def flip(b):
        bit = lax.rem(n // (1 << b), 2)
        return n + (1 - 2 * bit) * (1 << b)

    def held_at(b):
        base = n % (1 << (b + 1))
        return [base + i * (1 << (b + 1)) for i in range(n_node >> (b + 1))]

    def n_copy(j, q, b, slot):
        at = gath_ref.at[:, rows_of(j, q), :]
        return remote(at, at, nsend.at[j, slot], nrecv.at[j, q], {"node": flip(b)})

    def n_wait(j, q):
        n_copy(j, q, 0, 0).wait_recv()

    def hops(action, d):
        j = lax.rem(w + d, n_wide)
        slot = 0
        for b in reversed(range(bits)):
            for q in held_at(b):
                action(j, q, b, slot)
                slot += 1

    def first_hop(d):
        j = lax.rem(w + d, n_wide)
        x_copy(j, d, 0).wait_recv()
        x_copy(j, d, 1).wait_recv()
        n_copy(j, n, bits - 1, 0).start()

    out_refs = (mixed_ref, input_ref)

    def o_copy(t, src, to, d):
        at = out_refs[t].at[pl.ds(pl.multiple_of(src * piece, 16), piece), :]
        return remote(at, at, osend.at[t, d], orecv.at[t, src], {"node": to})

    def reduce_part(t):
        mine = pl.ds(pl.multiple_of(n * piece, 16), piece)
        acc = parts[t, mine, :].astype(jnp.float32)
        for d in range(1, n_node):
            src = lax.rem(n + d, n_node)
            p_copy(t, src, src, d).wait_recv()
            acc = acc + arrived[t, src].astype(jnp.float32)
        out_refs[t][mine, :] = acc.astype(jnp.bfloat16)
        for d in range(1, n_node):
            o_copy(t, n, lax.rem(n + d, n_node), d).start()

    for d in range(1, n_wide):
        first_hop(d)
    reduce_part(0)
    reduce_part(1)
    for d in range(1, n_wide):
        j = lax.rem(w + d, n_wide)
        slot = 1
        for b in reversed(range(bits - 1)):
            held = held_at(b)
            for q in held:
                @pl.when(lax.rem(q // (1 << (b + 1)), 2) != lax.rem(n // (1 << (b + 1)), 2))
                def _():
                    n_wait(j, q)
            for q in held:
                n_copy(j, q, b, slot).start()
                slot += 1
    last = [2 * i for i in range(n_node // 2)]
    for d in range(1, n_wide):
        j = lax.rem(w + d, n_wide)
        for i in last:
            n_wait(j, i + (1 - n % 2))
        h_copy(j, d).wait_recv()

    for t in range(2):
        for d in range(1, n_node):
            src = lax.rem(n + d, n_node)
            o_copy(t, src, src, d).wait_recv()
            o_copy(t, n, src, d).wait_send()
            p_copy(t, n, src, d).wait_send()
    for d in range(1, n_wide):
        x_copy(w, d, 0).wait_send()
        x_copy(w, d, 1).wait_send()
        h_copy(w, d).wait_send()
        hops(lambda j, q, b, slot: n_copy(j, q, b, slot).wait_send(), d)


    keep(0).wait()
    keep(1).wait()
    keep_acts.wait()


def main_call(inv, tokens, cotangent, blocks, n_wide, n_node):
    toks, width = tokens.shape
    dma = pltpu.SemaphoreType.DMA
    vmem = pl.BlockSpec(memory_space=pltpu.VMEM)
    smem = pl.BlockSpec(memory_space=pltpu.SMEM)
    hbm = pl.BlockSpec(memory_space=pl.ANY)
    bf16 = jnp.bfloat16
    return pl.pallas_call(
        functools.partial(main_kernel, n_wide, n_node),
        out_shape=(
            jax.ShapeDtypeStruct((toks, width), bf16),
            jax.ShapeDtypeStruct((toks, width), bf16),
            jax.ShapeDtypeStruct((2, n_wide * toks, width), bf16),
            jax.ShapeDtypeStruct((3, n_wide * toks, FF_DEV), bf16),
        ),
        in_specs=[smem, vmem, vmem, vmem],
        out_specs=(vmem, vmem, hbm, hbm),
        scratch_shapes=[
            pltpu.VMEM((3, width, FF_DEV), bf16),
            pltpu.VMEM((3, toks, FF_DEV), bf16),
            pltpu.VMEM((2, toks, width), bf16),
            pltpu.VMEM((2, n_node, toks // n_node, width), bf16),
            dma((n_wide, 2)), dma((n_wide, 2)), dma((n_wide, n_node)), dma((n_wide, n_node)),
            dma((n_wide,)), dma((n_wide,)), dma((2, n_node)), dma((2, n_node)), dma((2, n_node)), dma((2, n_node)),
            dma((3,)),
        ],
        compiler_params=pltpu.CompilerParams(
            collective_id=1, has_side_effects=True, vmem_limit_bytes=48 << 20
        ),
    )(inv, tokens, cotangent, blocks)


def grads_kernel(slots, rblocks, mine_ref, x_ref, acts_ref, out_ref, total):
    step = pl.program_id(0)
    per = rblocks * COLS

    @pl.when(step == 0)
    def _():
        total[...] = jnp.zeros_like(total)

    for s in range(slots):
        b = jnp.maximum(mine_ref[s], 0)
        m = b // per
        r = pl.multiple_of(((b // COLS) % rblocks) * EDGE, EDGE)
        c = pl.multiple_of((b % COLS) * EDGE, EDGE)
        total[s] += contract_tokens(x_ref[m // 2, :, pl.ds(r, EDGE)], acts_ref[m, :, pl.ds(c, EDGE)])

    @pl.when(step == pl.num_programs(0) - 1)
    def _():
        for s in range(slots):
            out_ref[s] = jnp.where(mine_ref[s] >= 0, total[s], 0.0).astype(out_ref.dtype)


def slot_grads(mine, gathered, acts, toks):
    slots = mine.shape[0]
    width = gathered.shape[2]
    return pl.pallas_call(
        functools.partial(grads_kernel, slots, width // EDGE),
        out_shape=jax.ShapeDtypeStruct((slots, EDGE, EDGE), jnp.bfloat16),
        grid_spec=pltpu.PrefetchScalarGridSpec(
            num_scalar_prefetch=1,
            grid=(gathered.shape[1] // toks,),
            in_specs=[
                pl.BlockSpec((2, toks, width), lambda j, ids: (0, j, 0)),
                pl.BlockSpec((3, toks, FF_DEV), lambda j, ids: (0, j, 0)),
            ],
            out_specs=pl.BlockSpec((slots, EDGE, EDGE), lambda j, ids: (0, 0, 0)),
            scratch_shapes=[pltpu.VMEM((slots, EDGE, EDGE), jnp.float32)],
        ),
        compiler_params=pltpu.CompilerParams(vmem_limit_bytes=24 << 20),
    )(mine, gathered, acts)


def per_device(n_wide, n_node, tokens, cotangent, tiles, tile_ids, tile_counts):
    slots = tiles.shape[2]
    ids = tile_ids.reshape(slots)
    mine = jnp.where(jnp.arange(slots, dtype=jnp.int32) < tile_counts[0, 0], ids, -1)
    padded = jnp.broadcast_to(jnp.pad(mine, (0, EDGE - slots), constant_values=-1)[None, :], (8, EDGE))
    gathered, all_ids = gather_tiles(tiles.reshape(slots * EDGE, EDGE), padded, n_wide)
    flat = all_ids[:, 0, :slots].reshape(1, n_wide * slots)
    numbers = jnp.arange(NBLK, dtype=jnp.int32)[:, None]
    none = n_wide * slots
    inv = jnp.min(jnp.where(flat == numbers, jnp.arange(none, dtype=jnp.int32)[None, :], none), axis=1)
    blocks = gathered.reshape(none + 1, EDGE, EDGE)
    mixed, input_grad, all_x, all_acts = main_call(inv, tokens, cotangent, blocks, n_wide, n_node)
    grads = slot_grads(mine, all_x, all_acts, tokens.shape[0])
    return mixed, input_grad, grads[None, None]


def solution(mesh):
    return jax.shard_map(
        functools.partial(per_device, mesh.shape["wide"], mesh.shape["node"]),
        mesh=mesh,
        in_specs=(
            P(("groups", "wide"), None),
            P(("groups", "wide"), None),
            P("node", "wide", None, None, None),
            P("node", "wide", None),
            P("node", "wide"),
        ),
        out_specs=(
            P(("groups", "wide"), None),
            P(("groups", "wide"), None),
            P(("groups", "node"), "wide", None, None, None),
        ),
        check_vma=False,
    )
```

time: 303 us -> 132 us (0.44)
  the two profiles are of different devices: /device:TPU:1 before, /device:TPU:9 now
where the time goes in v1:
time: 132 us
  Pallas kernels  121 us (92%)
  local copies, waits for them, and re-layouts  9.03 us (7%)
  between operations  1.33 us (1%)
    pallas_call x1, Pallas kernels, main_call(): pl.pallas_call(functools.partial(main_kernel, n_wide, n_node), out_shape=...  83 us
    pallas_call x1, Pallas kernels, gather_tiles(): pl.pallas_call(functools.partial(gather_kernel, n_wide, chunks), out_shap...  32.8 us
    unnamed x12, local copies, waits for them, and re-layouts  8.92 us
    pallas_call x1, Pallas kernels, slot_grads(): pl.pallas_call(functools.partial(grads_kernel, slots, width // EDGE), out...  4.85 us

profile of v1, /device:TPU:9, one launch (start us, length us, event | category | flops | bytes accessed | tf_op | source)
XLA Modules:
  0.0 131.8 jit_solution(6460512469273778946)
XLA Ops:
  1.3 0.7 compare_select_fusion.mine_ref
  1.9 0.0 copy-start.2
  2.0 1.1 copy-done.2
  3.1 32.8 %shard_map.76 = (bf16[12928,128]{1,0:T(8,128)(2,1)S(1)}, s32[4,8,128]{2,1,0:T(8,128)S(1)}) custom-call(bf16[3200,128]{1,0:T(8,128)(2,1)S(1)} %bitcast.8, s32[8,128]{1,0:T(8,128)S(1)} %broadcast_in_dim.28.ids_ref), custom_call_target="tpu_custom_call" | custom-call | tf_op jit(solution)/shard_map/pallas_call | solution.py:154
  35.9 0.0 copy-start.1
  35.9 1.7 %copy-done.1 = bf16[12928,128]{1,0:T(8,128)(2,1)} copy-done((bf16[12928,128]{1,0:T(8,128)(2,1)}, bf16[12928,128]{1,0:T(8,128)(2,1)S(1)}, u32[]{:S(2)}) %copy-start.1) | copy-done | bytes 3309592
  37.6 0.1 eq.15
  37.7 0.1 select_reduce_fusion.inv_ref
  37.8 0.0 copy-start.3
  37.8 1.1 copy-done.3
  38.8 0.0 copy-start.4
  38.8 1.1 copy-done.4
  39.9 83.0 %shard_map.77 = (bf16[128,2304]{1,0:T(8,128)(2,1)S(1)}, bf16[128,2304]{1,0:T(8,128)(2,1)S(1)}, bf16[2,512,2304]{2,1,0:T(8,128)(2,1)}, bf16[3,512,512]{2,1,0:T(8,128)(2,1)S(1)}) custom-call(s32[216]{0:T(256)S(1)} %select_reduce_fusion.inv_ref, bf16[128,2304]{1,0:T(8,128)(2,1)S(1)} %copy-done.3, bf16[128,2304]{1,0:T(8,128)(2,1)S(1)} %copy-done.4, ...), custom_call_target="tpu_custom_call" | custom-call | tf_op jit(solution)/shard_map/pallas_call | solution.py:350
  122.9 0.0 copy-start
  122.9 2.3 %copy-done = bf16[2,512,2304]{2,1,0:T(8,128)(2,1)S(1)} copy-done((bf16[2,512,2304]{2,1,0:T(8,128)(2,1)S(1)}, bf16[2,512,2304]{2,1,0:T(8,128)(2,1)}, u32[]{:S(2)}) %copy-start) | copy-done | bytes 4718616
  125.3 4.9 %shard_map.78 = bf16[25,128,128]{2,1,0:T(8,128)(2,1)} custom-call(s32[25]{0:T(128)S(1)} %compare_select_fusion.mine_ref, bf16[2,512,2304]{2,1,0:T(8,128)(2,1)S(1)} %copy-done, bf16[3,512,512]{2,1,0:T(8,128)(2,1)S(1)} %get-tuple-element.14.acts_ref), custom_call_target="tpu_custom_call" | custom-call | tf_op jit(solution)/shard_map/pallas_call | solution.py:399
  130.1 0.8 copy.11
  130.9 0.8 copy.12
  (3 shorter events, 0.0 us)
Async XLA Ops:
  1.9 1.1 copy-start.2
  35.9 1.7 %copy-start.1 = (bf16[12928,128]{1,0:T(8,128)(2,1)}, bf16[12928,128]{1,0:T(8,128)(2,1)S(1)}, u32[]{:S(2)}) copy-start(bf16[12928,128]{1,0:T(8,128)(2,1)S(1)} %get-tuple-element.10) | copy-start | bytes 9928708
  37.8 1.1 copy-start.3
  38.8 1.1 copy-start.4
  122.9 2.3 %copy-start = (bf16[2,512,2304]{2,1,0:T(8,128)(2,1)S(1)}, bf16[2,512,2304]{2,1,0:T(8,128)(2,1)}, u32[]{:S(2)}) copy-start(bf16[2,512,2304]{2,1,0:T(8,128)(2,1)} %get-tuple-element.13.x_ref) | copy-start | bytes 14155780

commit v2 on v1

--- a/solution.py
+++ b/solution.py
@@ -199,16 +199,71 @@
     keep(1).start()
     pl.semaphore_wait(barrier, n_wide + n_node - 2)
 
-    def x_copy(j, d, t):
+    def both_ways(d, action):
+        for way in (1, -1):
+            j = w - d * way
+            have = (j >= 0) if way > 0 else (j < n_wide)
+            more = (w < n_wide - 1) if way > 0 else (w > 0)
+            action(j, way, have, more)
+
+    def x_copy(j, way, t, own=False):
+        to = gath_ref.at[t, rows_of(j, n), :]
         mine = (tok_ref, cot_ref)[t].at[pl.ds(pl.multiple_of(n * piece, 16), piece), :]
         return remote(
-            mine, gath_ref.at[t, rows_of(j, n), :], xsend.at[d, t], xrecv.at[j, t],
-            {"wide": lax.rem(w + d, n_wide)},
+            mine if own else to, to, xsend.at[0 if way > 0 else 1, j, t], xrecv.at[j, t], {"wide": w + way}
         )
 
-    for d in range(1, n_wide):
-        for t in range(2):
-            x_copy(w, d, t).start()
+    def x_begin(j, way, have, more):
+        @pl.when(more)
+        def _():
+            for t in range(2):
+                x_copy(j, way, t, True).start()
+
+    def x_pass(j, way, have, more):
+        @pl.when(have)
+        def _():
+            for t in range(2):
+                x_copy(j, way, t).wait_recv()
+
+        @pl.when(have & more)
+        def _():
+            for t in range(2):
+                x_copy(j, way, t).start()
+
+        @pl.when(have)
+        def _():
+            n_copy(j, n, bits - 1, 0).start()
+
+    def x_sent(j, way, have, more):
+        @pl.when(have & more)
+        def _():
+            for t in range(2):
+                x_copy(j, way, t).wait_send()
+
+    def flip(b):
+        bit = lax.rem(n // (1 << b), 2)
+        return n + (1 - 2 * bit) * (1 << b)
+
+    def held_at(b):
+        base = n % (1 << (b + 1))
+        return [base + i * (1 << (b + 1)) for i in range(n_node >> (b + 1))]
+
+    def n_copy(j, q, b, slot):
+        at = gath_ref.at[:, rows_of(j, q), :]
+        return remote(at, at, nsend.at[j, slot], nrecv.at[j, q], {"node": flip(b)})
+
+    def n_wait(j, q):
+        n_copy(j, q, 0, 0).wait_recv()
+
+    def hops(action, d):
+        j = lax.rem(w + d, n_wide)
+        slot = 0
+        for b in reversed(range(bits)):
+            for q in held_at(b):
+                action(j, q, b, slot)
+                slot += 1
+
+    both_ways(0, x_begin)
 
     def place(r, _):
         for m in range(3):
@@ -221,6 +276,7 @@
 
     gate = jnp.dot(tok_ref[...], weights[0], preferred_element_type=jnp.float32)
     up = jnp.dot(tok_ref[...], weights[1], preferred_element_type=jnp.float32)
+    both_ways(1, x_pass)
     value, slope = gelu_parts(gate)
     hidden = (value * up).astype(jnp.bfloat16)
     hidden_grad = jnp.dot(cot_ref[...], weights[2], preferred_element_type=jnp.float32)
@@ -232,12 +288,32 @@
     keep_acts = pltpu.make_async_copy(acts, acts_ref.at[:, own_rows, :], ssem.at[2])
     keep_acts.start()
 
-    def h_copy(j, d):
+    def h_copy(j, way, own=False):
         at = acts_ref.at[:, pl.ds(pl.multiple_of(j * toks, 16), toks), :]
-        return remote(acts, at, hsend.at[d], hrecv.at[j], {"wide": lax.rem(w + d, n_wide)})
-
-    for d in range(1, n_wide):
-        h_copy(w, d).start()
+        return remote(
+            acts if own else at, at, hsend.at[0 if way > 0 else 1, j], hrecv.at[j], {"wide": w + way}
+        )
+
+    def h_begin(j, way, have, more):
+        @pl.when(more)
+        def _():
+            h_copy(j, way, True).start()
+
+    def h_pass(j, way, have, more):
+        @pl.when(have)
+        def _():
+            h_copy(j, way).wait_recv()
+
+        @pl.when(have & more)
+        def _():
+            h_copy(j, way).start()
+
+    def h_sent(j, way, have, more):
+        @pl.when(have & more)
+        def _():
+            h_copy(j, way).wait_send()
+
+    both_ways(0, h_begin)
 
     def p_copy(t, src, to, d):
         return remote(
@@ -249,38 +325,11 @@
     parts[0] = out_part.astype(jnp.bfloat16)
     for d in range(1, n_node):
         p_copy(0, n, lax.rem(n + d, n_node), d).start()
+    if n_wide > 2:
+        both_ways(2, x_pass)
     parts[1] = (contract_rows(gate_grad, weights[0]) + contract_rows(up_grad, weights[1])).astype(jnp.bfloat16)
     for d in range(1, n_node):
         p_copy(1, n, lax.rem(n + d, n_node), d).start()
-
-    def flip(b):
-        bit = lax.rem(n // (1 << b), 2)
-        return n + (1 - 2 * bit) * (1 << b)
-
-    def held_at(b):
-        base = n % (1 << (b + 1))
-        return [base + i * (1 << (b + 1)) for i in range(n_node >> (b + 1))]
-
-    def n_copy(j, q, b, slot):
-        at = gath_ref.at[:, rows_of(j, q), :]
-        return remote(at, at, nsend.at[j, slot], nrecv.at[j, q], {"node": flip(b)})
-
-    def n_wait(j, q):
-        n_copy(j, q, 0, 0).wait_recv()
-
-    def hops(action, d):
-        j = lax.rem(w + d, n_wide)
-        slot = 0
-        for b in reversed(range(bits)):
-            for q in held_at(b):
-                action(j, q, b, slot)
-                slot += 1
-
-    def first_hop(d):
-        j = lax.rem(w + d, n_wide)
-        x_copy(j, d, 0).wait_recv()
-        x_copy(j, d, 1).wait_recv()
-        n_copy(j, n, bits - 1, 0).start()
 
     out_refs = (mixed_ref, input_ref)
 
@@ -299,9 +348,11 @@
         for d in range(1, n_node):
             o_copy(t, n, lax.rem(n + d, n_node), d).start()
 
-    for d in range(1, n_wide):
-        first_hop(d)
+    both_ways(1, h_pass)
     reduce_part(0)
+    for d in range(3, n_wide):
+        both_ways(d, x_pass)
+        both_ways(d - 1, h_pass)
     reduce_part(1)
     for d in range(1, n_wide):
         j = lax.rem(w + d, n_wide)
@@ -320,7 +371,7 @@
         j = lax.rem(w + d, n_wide)
         for i in last:
             n_wait(j, i + (1 - n % 2))
-        h_copy(j, d).wait_recv()
+    both_ways(n_wide - 1, h_pass)
 
     for t in range(2):
         for d in range(1, n_node):
@@ -329,12 +380,12 @@
             o_copy(t, n, src, d).wait_send()
             p_copy(t, n, src, d).wait_send()
     for d in range(1, n_wide):
-        x_copy(w, d, 0).wait_send()
-        x_copy(w, d, 1).wait_send()
-        h_copy(w, d).wait_send()
         hops(lambda j, q, b, slot: n_copy(j, q, b, slot).wait_send(), d)
 
 
+    for d in range(n_wide):
+        both_ways(d, x_sent)
+        both_ways(d, h_sent)
     keep(0).wait()
     keep(1).wait()
     keep_acts.wait()
@@ -362,8 +413,8 @@
             pltpu.VMEM((3, toks, FF_DEV), bf16),
             pltpu.VMEM((2, toks, width), bf16),
             pltpu.VMEM((2, n_node, toks // n_node, width), bf16),
-            dma((n_wide, 2)), dma((n_wide, 2)), dma((n_wide, n_node)), dma((n_wide, n_node)),
-            dma((n_wide,)), dma((n_wide,)), dma((2, n_node)), dma((2, n_node)), dma((2, n_node)), dma((2, n_node)),
+            dma((2, n_wide, 2)), dma((n_wide, 2)), dma((n_wide, n_node)), dma((n_wide, n_node)),
+            dma((2, n_wide)), dma((n_wide,)), dma((2, n_node)), dma((2, n_node)), dma((2, n_node)), dma((2, n_node)),
             dma((3,)),
         ],
         compiler_params=pltpu.CompilerParams(

time: 132 us -> 111 us (0.84)
  the two profiles are of different devices: /device:TPU:9 before, /device:TPU:1 now
where the time goes in v2:
time: 111 us; the launch traced here: 110 us
  Pallas kernels  98.5 us (89%)
  local copies, waits for them, and re-layouts  9.03 us (8%)
  between operations  1.33 us (1%)
    pallas_call x1, Pallas kernels, main_call(): pl.pallas_call(functools.partial(main_kernel, n_wide, n_node), out_shape=...  57.7 us
    pallas_call x1, Pallas kernels, gather_tiles(): pl.pallas_call(functools.partial(gather_kernel, n_wide, chunks), out_shap...  36 us
    unnamed x12, local copies, waits for them, and re-layouts  8.92 us
    pallas_call x1, Pallas kernels, slot_grads(): pl.pallas_call(functools.partial(grads_kernel, slots, width // EDGE), out...  4.89 us

profile of v2, /device:TPU:1, one launch (start us, length us, event | category | flops | bytes accessed | tf_op | source)
XLA Modules:
  0.0 109.7 jit_solution(9893360031007417660)
XLA Ops:
  1.3 0.7 compare_select_fusion.mine_ref
  1.9 0.0 copy-start.2
  2.0 1.1 %copy-done.2 = bf16[1,1,25,128,128]{4,3,2,1,0:T(8,128)(2,1)S(1)} copy-done((bf16[1,1,25,128,128]{4,3,2,1,0:T(8,128)(2,1)S(1)}, bf16[1,1,25,128,128]{4,3,2,1,0:T(8,128)(2,1)}, u32[]{:S(2)}) %copy-start.2) | copy-done | bytes 819224
  3.1 36.0 %shard_map.76 = (bf16[12928,128]{1,0:T(8,128)(2,1)S(1)}, s32[4,8,128]{2,1,0:T(8,128)S(1)}) custom-call(bf16[3200,128]{1,0:T(8,128)(2,1)S(1)} %bitcast.8, s32[8,128]{1,0:T(8,128)S(1)} %broadcast_in_dim.28.ids_ref), custom_call_target="tpu_custom_call" | custom-call | tf_op jit(solution)/shard_map/pallas_call | solution.py:154
  39.1 0.0 copy-start.1
  39.1 1.7 %copy-done.1 = bf16[12928,128]{1,0:T(8,128)(2,1)} copy-done((bf16[12928,128]{1,0:T(8,128)(2,1)}, bf16[12928,128]{1,0:T(8,128)(2,1)S(1)}, u32[]{:S(2)}) %copy-start.1) | copy-done | bytes 3309592
  40.8 0.1 eq.15
  40.9 0.1 select_reduce_fusion.inv_ref
  41.0 0.0 copy-start.3
  41.0 1.1 copy-done.3
  42.1 0.0 copy-start.4
  42.1 1.1 copy-done.4
  43.1 57.7 %shard_map.77 = (bf16[128,2304]{1,0:T(8,128)(2,1)S(1)}, bf16[128,2304]{1,0:T(8,128)(2,1)S(1)}, bf16[2,512,2304]{2,1,0:T(8,128)(2,1)}, bf16[3,512,512]{2,1,0:T(8,128)(2,1)S(1)}) custom-call(s32[216]{0:T(256)S(1)} %select_reduce_fusion.inv_ref, bf16[128,2304]{1,0:T(8,128)(2,1)S(1)} %copy-done.3, bf16[128,2304]{1,0:T(8,128)(2,1)S(1)} %copy-done.4, ...), custom_call_target="tpu_custom_call" | custom-call | tf_op jit(solution)/shard_map/pallas_call | solution.py:401
  100.8 0.0 copy-start
  100.8 2.3 %copy-done = bf16[2,512,2304]{2,1,0:T(8,128)(2,1)S(1)} copy-done((bf16[2,512,2304]{2,1,0:T(8,128)(2,1)S(1)}, bf16[2,512,2304]{2,1,0:T(8,128)(2,1)}, u32[]{:S(2)}) %copy-start) | copy-done | bytes 4718616
  103.1 4.9 %shard_map.78 = bf16[25,128,128]{2,1,0:T(8,128)(2,1)} custom-call(s32[25]{0:T(128)S(1)} %compare_select_fusion.mine_ref, bf16[2,512,2304]{2,1,0:T(8,128)(2,1)S(1)} %copy-done, bf16[3,512,512]{2,1,0:T(8,128)(2,1)S(1)} %get-tuple-element.14.acts_ref), custom_call_target="tpu_custom_call" | custom-call | tf_op jit(solution)/shard_map/pallas_call | solution.py:450
  108.0 0.8 copy.11
  108.8 0.8 copy.12
  (3 shorter events, 0.0 us)
Async XLA Ops:
  1.9 1.1 %copy-start.2 = (bf16[1,1,25,128,128]{4,3,2,1,0:T(8,128)(2,1)S(1)}, bf16[1,1,25,128,128]{4,3,2,1,0:T(8,128)(2,1)}, u32[]{:S(2)}) copy-start(bf16[1,1,25,128,128]{4,3,2,1,0:T(8,128)(2,1)} %param.7) | copy-start | bytes 2457604
  39.1 1.7 %copy-start.1 = (bf16[12928,128]{1,0:T(8,128)(2,1)}, bf16[12928,128]{1,0:T(8,128)(2,1)S(1)}, u32[]{:S(2)}) copy-start(bf16[12928,128]{1,0:T(8,128)(2,1)S(1)} %get-tuple-element.10) | copy-start | bytes 9928708
  41.0 1.1 copy-start.3
  42.1 1.1 copy-start.4
  100.8 2.3 %copy-start = (bf16[2,512,2304]{2,1,0:T(8,128)(2,1)S(1)}, bf16[2,512,2304]{2,1,0:T(8,128)(2,1)}, u32[]{:S(2)}) copy-start(bf16[2,512,2304]{2,1,0:T(8,128)(2,1)} %get-tuple-element.13.x_ref) | copy-start | bytes 14155780

commit v3 on v2

--- a/solution.py
+++ b/solution.py
@@ -9,7 +9,6 @@
 from jax.sharding import PartitionSpec as P
 
 FF_DEV = 512
-NBLK = 216
 EDGE = 128
 COLS = FF_DEV // EDGE
 MESH = pl.DeviceIdType.MESH
@@ -45,137 +44,19 @@
     )
 
 
-def gather_kernel(n_wide, chunks, tiles_ref, ids_ref, all_ref, allids_ref,
-                  zsend, zrecv, ysend, yrecv, isend, irecv, own_sem):
-    w = lax.axis_index("wide")
-    g = lax.axis_index("groups")
-    other = 1 - g
-    rows = tiles_ref.shape[0]
-    half = rows // 2
-    step = half // chunks
-
-    barrier = pltpu.get_barrier_semaphore()
-    for d in range(1, n_wide):
-        pl.semaphore_signal(barrier, inc=1, device_id={"wide": lax.rem(w + d, n_wide)}, device_id_type=MESH)
-    pl.semaphore_signal(barrier, inc=1, device_id={"groups": other}, device_id_type=MESH)
-    own = pltpu.make_async_copy(tiles_ref, all_ref.at[pl.ds(pl.multiple_of(w * rows, 16), rows)], own_sem)
-    own.start()
-    all_ref[n_wide * rows:, :] = jnp.zeros((EDGE, EDGE), all_ref.dtype)
-    allids_ref[w] = ids_ref[...]
-    pl.semaphore_wait(barrier, n_wide)
-
-    def part(group, k):
-        return pl.ds(pl.multiple_of(group * half + k * step, 16), step)
-
-    def piece(j, group, k):
-        return all_ref.at[pl.ds(pl.multiple_of(j * rows + group * half + k * step, 16), step)]
-
-    def z_copy(j, k, way):
-        return remote(
-            piece(j, g, k), piece(j, g, k),
-            zsend.at[0 if way > 0 else 1, j, k], zrecv.at[j, k], {"wide": w + way},
-        )
-
-    def z_own(k, way):
-        return remote(
-            tiles_ref.at[part(g, k)], piece(w, g, k),
-            zsend.at[0 if way > 0 else 1, w, k], zrecv.at[w, k], {"wide": w + way},
-        )
-
-    def y_copy(j, k, group):
-        return remote(
-            piece(j, group, k), piece(j, group, k),
-            ysend.at[j, k], yrecv.at[j, k], {"groups": other},
-        )
-
-    def ids_copy(d):
-        to = lax.rem(w + d, n_wide)
-        return remote(allids_ref.at[w], allids_ref.at[w], isend.at[d], irecv.at[w], {"wide": to})
-
-    right = w < n_wide - 1
-    left = w > 0
-    for k in range(chunks):
-        @pl.when(right)
-        def _():
-            z_own(k, 1).start()
-
-        @pl.when(left)
-        def _():
-            z_own(k, -1).start()
-    for d in range(1, n_wide):
-        ids_copy(d).start()
-    for d in range(1, n_wide):
-        for k in range(chunks):
-            for way in (1, -1):
-                j = w - d * way
-                have = (j >= 0) if way > 0 else (j < n_wide)
-
-                @pl.when(have)
-                def _():
-                    z_copy(j, k, way).wait_recv()
-
-                @pl.when(have & (right if way > 0 else left))
-                def _():
-                    z_copy(j, k, way).start()
-
-                @pl.when(have)
-                def _():
-                    y_copy(j, k, g).start()
-    own.wait()
-    for k in range(chunks):
-        @pl.when(right)
-        def _():
-            z_own(k, 1).wait_send()
-
-        @pl.when(left)
-        def _():
-            z_own(k, -1).wait_send()
-    for d in range(1, n_wide):
-        ids_copy(d).wait_send()
-        j = lax.rem(w + d, n_wide)
-        remote(allids_ref.at[j], allids_ref.at[j], isend.at[d], irecv.at[j], {"wide": j}).wait_recv()
-        for k in range(chunks):
-            y_copy(j, k, g).wait_send()
-            y_copy(j, k, other).wait_recv()
-            for way in (1, -1):
-                i = w - d * way
-                have = (i >= 0) if way > 0 else (i < n_wide)
-
-                @pl.when(have & (right if way > 0 else left))
-                def _():
-                    z_copy(i, k, way).wait_send()
-
-
-def gather_tiles(tiles, ids, n_wide):
-    rows = tiles.shape[0]
-    chunks = 5 if (rows // 2) % 80 == 0 else 1
-    dma = pltpu.SemaphoreType.DMA
-    vmem = pl.BlockSpec(memory_space=pltpu.VMEM)
-    return pl.pallas_call(
-        functools.partial(gather_kernel, n_wide, chunks),
-        out_shape=(
-            jax.ShapeDtypeStruct((n_wide * rows + EDGE, EDGE), tiles.dtype),
-            jax.ShapeDtypeStruct((n_wide,) + ids.shape, ids.dtype),
-        ),
-        in_specs=[vmem, vmem],
-        out_specs=(vmem, vmem),
-        scratch_shapes=[
-            dma((2, n_wide, chunks)), dma((n_wide, chunks)), dma((n_wide, chunks)), dma((n_wide, chunks)),
-            dma((n_wide,)), dma((n_wide,)), dma,
-        ],
-        compiler_params=pltpu.CompilerParams(
-            collective_id=0, has_side_effects=True, vmem_limit_bytes=40 << 20
-        ),
-    )(tiles, ids)
-
-
-def main_kernel(n_wide, n_node,
-                inv_ref, tok_ref, cot_ref, tiles_ref,
+def main_kernel(n_wide, n_node, chunks,
+                ids_ref, tok_ref, cot_ref, tiles_ref,
                 mixed_ref, input_ref, gath_ref, acts_ref,
-                weights, acts, parts, arrived,
+                blocks, all_ids, ids_now, inv_vec, inv_ref, weights, acts, parts, arrived,
+                zsend, zrecv, ysend, yrecv, isend, irecv, lsem,
                 xsend, xrecv, nsend, nrecv, hsend, hrecv, psend, precv, osend, orecv, ssem):
     w = lax.axis_index("wide")
     n = lax.axis_index("node")
+    g = lax.axis_index("groups")
+    other = 1 - g
+    slots = tiles_ref.shape[0]
+    step = slots // chunks
+    none = n_wide * slots
     toks, width = tok_ref.shape
     piece = toks // n_node
     rblocks = width // EDGE
@@ -188,6 +69,12 @@
     for d in range(1, n_node):
         pl.semaphore_signal(barrier, inc=1, device_id={"node": lax.rem(n + d, n_node)}, device_id_type=MESH)
 
+    pl.semaphore_signal(barrier, inc=1, device_id={"groups": other}, device_id_type=MESH)
+    own_tiles = pltpu.make_async_copy(tiles_ref, blocks.at[pl.ds(w * slots, slots)], lsem.at[0])
+    own_tiles.start()
+    blocks[none] = jnp.zeros((EDGE, EDGE), blocks.dtype)
+    all_ids[w] = ids_ref[...]
+
     def rows_of(j, q):
         return pl.ds(pl.multiple_of(j * toks + q * piece, 16), piece)
 
@@ -197,7 +84,7 @@
 
     keep(0).start()
     keep(1).start()
-    pl.semaphore_wait(barrier, n_wide + n_node - 2)
+    pl.semaphore_wait(barrier, n_wide + n_node - 1)
 
     def both_ways(d, action):
         for way in (1, -1):
@@ -205,6 +92,53 @@
             have = (j >= 0) if way > 0 else (j < n_wide)
             more = (w < n_wide - 1) if way > 0 else (w > 0)
             action(j, way, have, more)
+
+    half = EDGE // 2
+
+    def piece_of(j, group, k):
+        return blocks.at[pl.ds(j * slots + k * step, step), pl.ds(pl.multiple_of(group * half, half), half), :]
+
+    def z_copy(j, k, way, own=False):
+        mine = tiles_ref.at[pl.ds(k * step, step), pl.ds(pl.multiple_of(g * half, half), half), :]
+        to = piece_of(j, g, k)
+        return remote(
+            mine if own else to, to, zsend.at[0 if way > 0 else 1, j, k], zrecv.at[j, k], {"wide": w + way}
+        )
+
+    def y_copy(j, k, group):
+        at = piece_of(j, group, k)
+        return remote(at, at, ysend.at[j, k], yrecv.at[j, k], {"groups": other})
+
+    def ids_copy(j, d, to):
+        return remote(all_ids.at[j], all_ids.at[j], isend.at[d], irecv.at[j], {"wide": to})
+
+    def z_pass(k):
+        def go(j, way, have, more):
+            @pl.when(have)
+            def _():
+                z_copy(j, k, way).wait_recv()
+
+            @pl.when(have & more)
+            def _():
+                z_copy(j, k, way).start()
+
+            @pl.when(have)
+            def _():
+                y_copy(j, k, g).start()
+        return go
+
+    def z_sent(j, way, have, more):
+        @pl.when(have & more)
+        def _():
+            for k in range(chunks):
+                z_copy(j, k, way).wait_send()
+
+    def z_begin(k):
+        def go(j, way, have, more):
+            @pl.when(more)
+            def _():
+                z_copy(j, k, way, True).start()
+        return go
 
     def x_copy(j, way, t, own=False):
         to = gath_ref.at[t, rows_of(j, n), :]
@@ -263,20 +197,54 @@
                 action(j, q, b, slot)
                 slot += 1
 
+    for k in range(chunks):
+        both_ways(0, z_begin(k))
+    for d in range(1, n_wide):
+        ids_copy(w, d, lax.rem(w + d, n_wide)).start()
+    for d in range(1, n_wide - 1):
+        for k in range(chunks):
+            both_ways(d, z_pass(k))
     both_ways(0, x_begin)
+
+    for d in range(1, n_wide):
+        j = lax.rem(w + d, n_wide)
+        ids_copy(j, d, j).wait_recv()
+    ids_in = pltpu.make_async_copy(all_ids, ids_now, lsem.at[1])
+    ids_in.start()
+    ids_in.wait()
+    number = lax.broadcasted_iota(jnp.int32, (8, EDGE), 0) * EDGE + lax.broadcasted_iota(jnp.int32, (8, EDGE), 1)
+
+    def add_ids(j, found):
+        for s in range(slots):
+            hit = jnp.maximum(1 - jnp.abs(number - ids_now[j, 0, s]), 0)
+            found = jnp.minimum(found, none + hit * (j * slots + s - none))
+        return found
+
+    inv_vec[...] = lax.fori_loop(0, n_wide, add_ids, jnp.full((8, EDGE), none, jnp.int32))
+    inv_in = pltpu.make_async_copy(inv_vec, inv_ref, lsem.at[2])
+    inv_in.start()
+    inv_in.wait()
+
+    for k in range(chunks):
+        both_ways(n_wide - 1, z_pass(k))
+    for d in range(1, n_wide):
+        for k in range(chunks):
+            y_copy(lax.rem(w + d, n_wide), k, other).wait_recv()
+    own_tiles.wait()
 
     def place(r, _):
         for m in range(3):
             for c in range(COLS):
-                i = inv_ref[m * per + r * COLS + c]
-                weights[m, pl.ds(pl.multiple_of(r * EDGE, EDGE), EDGE), c * EDGE:(c + 1) * EDGE] = tiles_ref[i]
+                b = m * per + r * COLS + c
+                i = inv_ref[b // EDGE, b % EDGE]
+                weights[m, pl.ds(pl.multiple_of(r * EDGE, EDGE), EDGE), c * EDGE:(c + 1) * EDGE] = blocks[i]
         return 0
 
     lax.fori_loop(0, rblocks, place, 0)
+    both_ways(1, x_pass)
 
     gate = jnp.dot(tok_ref[...], weights[0], preferred_element_type=jnp.float32)
     up = jnp.dot(tok_ref[...], weights[1], preferred_element_type=jnp.float32)
-    both_ways(1, x_pass)
     value, slope = gelu_parts(gate)
     hidden = (value * up).astype(jnp.bfloat16)
     hidden_grad = jnp.dot(cot_ref[...], weights[2], preferred_element_type=jnp.float32)
@@ -386,33 +354,47 @@
     for d in range(n_wide):
         both_ways(d, x_sent)
         both_ways(d, h_sent)
+        both_ways(d, z_sent)
+    for d in range(1, n_wide):
+        j = lax.rem(w + d, n_wide)
+        ids_copy(w, d, j).wait_send()
+        for k in range(chunks):
+            y_copy(j, k, g).wait_send()
     keep(0).wait()
     keep(1).wait()
     keep_acts.wait()
 
 
-def main_call(inv, tokens, cotangent, blocks, n_wide, n_node):
+def main_call(ids, tokens, cotangent, tiles, n_wide, n_node):
     toks, width = tokens.shape
     dma = pltpu.SemaphoreType.DMA
     vmem = pl.BlockSpec(memory_space=pltpu.VMEM)
-    smem = pl.BlockSpec(memory_space=pltpu.SMEM)
+    slots = tiles.shape[0]
+    chunks = 5 if slots % 5 == 0 else 1
     hbm = pl.BlockSpec(memory_space=pl.ANY)
     bf16 = jnp.bfloat16
     return pl.pallas_call(
-        functools.partial(main_kernel, n_wide, n_node),
+        functools.partial(main_kernel, n_wide, n_node, chunks),
         out_shape=(
             jax.ShapeDtypeStruct((toks, width), bf16),
             jax.ShapeDtypeStruct((toks, width), bf16),
             jax.ShapeDtypeStruct((2, n_wide * toks, width), bf16),
             jax.ShapeDtypeStruct((3, n_wide * toks, FF_DEV), bf16),
         ),
-        in_specs=[smem, vmem, vmem, vmem],
+        in_specs=[vmem, vmem, vmem, vmem],
         out_specs=(vmem, vmem, hbm, hbm),
         scratch_shapes=[
+            pltpu.VMEM((n_wide * slots + 1, EDGE, EDGE), bf16),
+            pltpu.VMEM((n_wide, 8, EDGE), jnp.int32),
+            pltpu.SMEM((n_wide, 8, EDGE), jnp.int32),
+            pltpu.VMEM((8, EDGE), jnp.int32),
+            pltpu.SMEM((8, EDGE), jnp.int32),
             pltpu.VMEM((3, width, FF_DEV), bf16),
             pltpu.VMEM((3, toks, FF_DEV), bf16),
             pltpu.VMEM((2, toks, width), bf16),
             pltpu.VMEM((2, n_node, toks // n_node, width), bf16),
+            dma((2, n_wide, chunks)), dma((n_wide, chunks)), dma((n_wide, chunks)), dma((n_wide, chunks)),
+            dma((n_wide,)), dma((n_wide,)), dma((3,)),
             dma((2, n_wide, 2)), dma((n_wide, 2)), dma((n_wide, n_node)), dma((n_wide, n_node)),
             dma((2, n_wide)), dma((n_wide,)), dma((2, n_node)), dma((2, n_node)), dma((2, n_node)), dma((2, n_node)),
             dma((3,)),
@@ -420,7 +402,7 @@
         compiler_params=pltpu.CompilerParams(
             collective_id=1, has_side_effects=True, vmem_limit_bytes=48 << 20
         ),
-    )(inv, tokens, cotangent, blocks)
+    )(ids, tokens, cotangent, tiles)
 
 
 def grads_kernel(slots, rblocks, mine_ref, x_ref, acts_ref, out_ref, total):
@@ -469,13 +451,9 @@
     ids = tile_ids.reshape(slots)
     mine = jnp.where(jnp.arange(slots, dtype=jnp.int32) < tile_counts[0, 0], ids, -1)
     padded = jnp.broadcast_to(jnp.pad(mine, (0, EDGE - slots), constant_values=-1)[None, :], (8, EDGE))
-    gathered, all_ids = gather_tiles(tiles.reshape(slots * EDGE, EDGE), padded, n_wide)
-    flat = all_ids[:, 0, :slots].reshape(1, n_wide * slots)
-    numbers = jnp.arange(NBLK, dtype=jnp.int32)[:, None]
-    none = n_wide * slots
-    inv = jnp.min(jnp.where(flat == numbers, jnp.arange(none, dtype=jnp.int32)[None, :], none), axis=1)
-    blocks = gathered.reshape(none + 1, EDGE, EDGE)
-    mixed, input_grad, all_x, all_acts = main_call(inv, tokens, cotangent, blocks, n_wide, n_node)
+    mixed, input_grad, all_x, all_acts = main_call(
+        padded, tokens, cotangent, tiles.reshape(slots, EDGE, EDGE), n_wide, n_node
+    )
     grads = slot_grads(mine, all_x, all_acts, tokens.shape[0])
     return mixed, input_grad, grads[None, None]
 

time: 111 us -> 101 us (0.910)
  Pallas kernels: 98.5 us -> 91.2 us
  local copies, waits for them, and re-layouts: 9.03 us -> 7.24 us
    pallas_call x2 -> x1, Pallas kernels: 93.6 us -> 86.3 us  [main_call(): pl.pallas_call(functools.partial(main_kernel, n_wide, n_node, chunks), ou...]
    unnamed x12 -> x10, local copies, waits for them, and re-layouts: 8.92 us -> 7.23 us
where the time goes in v3:
time: 101 us; the launch traced here: 100 us
  Pallas kernels  91.2 us (90%)
  local copies, waits for them, and re-layouts  7.24 us (7%)
  between operations  1.3 us (1%)
    pallas_call x1, Pallas kernels, main_call(): pl.pallas_call(functools.partial(main_kernel, n_wide, n_node, chunks), ou...  86.3 us
    unnamed x10, local copies, waits for them, and re-layouts  7.23 us
    pallas_call x1, Pallas kernels, slot_grads(): pl.pallas_call(functools.partial(grads_kernel, slots, width // EDGE), out...  4.89 us

profile of v3, /device:TPU:1, one launch (start us, length us, event | category | flops | bytes accessed | tf_op | source)
XLA Modules:
  0.0 100.4 jit_solution(16941563275750402511)
XLA Ops:
  1.3 0.7 compare_select_fusion.mine_ref
  1.9 0.0 copy-start.1
  2.0 1.1 %copy-done.1 = bf16[1,1,25,128,128]{4,3,2,1,0:T(8,128)(2,1)S(1)} copy-done((bf16[1,1,25,128,128]{4,3,2,1,0:T(8,128)(2,1)S(1)}, bf16[1,1,25,128,128]{4,3,2,1,0:T(8,128)(2,1)}, u32[]{:S(2)}) %copy-start.1) | copy-done | bytes 819224
  3.1 0.0 copy-start.2
  3.1 1.1 %copy-done.2 = bf16[128,2304]{1,0:T(8,128)(2,1)S(1)} copy-done((bf16[128,2304]{1,0:T(8,128)(2,1)S(1)}, bf16[128,2304]{1,0:T(8,128)(2,1)}, u32[]{:S(2)}) %copy-start.2) | copy-done | bytes 589848
  4.2 0.0 copy-start.3
  4.2 1.1 %copy-done.3 = bf16[128,2304]{1,0:T(8,128)(2,1)S(1)} copy-done((bf16[128,2304]{1,0:T(8,128)(2,1)S(1)}, bf16[128,2304]{1,0:T(8,128)(2,1)}, u32[]{:S(2)}) %copy-start.3) | copy-done | bytes 589848
  5.2 86.3 %shard_map.76 = (bf16[128,2304]{1,0:T(8,128)(2,1)S(1)}, bf16[128,2304]{1,0:T(8,128)(2,1)S(1)}, bf16[2,512,2304]{2,1,0:T(8,128)(2,1)}, bf16[3,512,512]{2,1,0:T(8,128)(2,1)S(1)}) custom-call(s32[8,128]{1,0:T(8,128)S(1)} %broadcast_in_dim.14.ids_ref, bf16[128,2304]{1,0:T(8,128)(2,1)S(1)} %copy-done.2, bf16[128,2304]{1,0:T(8,128)(2,1)S(1)} %copy-done.3, ...), custom_call_target="tpu_custom_call" | custom-call | tf_op jit(solution)/shard_map/pallas_call | solution.py:376
  91.6 0.0 copy-start
  91.6 2.3 %copy-done = bf16[2,512,2304]{2,1,0:T(8,128)(2,1)S(1)} copy-done((bf16[2,512,2304]{2,1,0:T(8,128)(2,1)S(1)}, bf16[2,512,2304]{2,1,0:T(8,128)(2,1)}, u32[]{:S(2)}) %copy-start) | copy-done | bytes 4718616
  93.9 4.9 %shard_map.77 = bf16[25,128,128]{2,1,0:T(8,128)(2,1)} custom-call(s32[25]{0:T(128)S(1)} %compare_select_fusion.mine_ref, bf16[2,512,2304]{2,1,0:T(8,128)(2,1)S(1)} %copy-done, bf16[3,512,512]{2,1,0:T(8,128)(2,1)S(1)} %get-tuple-element.10.acts_ref), custom_call_target="tpu_custom_call" | custom-call | tf_op jit(solution)/shard_map/pallas_call | solution.py:432
  98.8 0.8 copy.11
  99.6 0.8 copy.12
  (2 shorter events, 0.0 us)
Async XLA Ops:
  1.9 1.1 %copy-start.1 = (bf16[1,1,25,128,128]{4,3,2,1,0:T(8,128)(2,1)S(1)}, bf16[1,1,25,128,128]{4,3,2,1,0:T(8,128)(2,1)}, u32[]{:S(2)}) copy-start(bf16[1,1,25,128,128]{4,3,2,1,0:T(8,128)(2,1)} %param.7) | copy-start | bytes 2457604
  3.1 1.1 %copy-start.2 = (bf16[128,2304]{1,0:T(8,128)(2,1)S(1)}, bf16[128,2304]{1,0:T(8,128)(2,1)}, u32[]{:S(2)}) copy-start(bf16[128,2304]{1,0:T(8,128)(2,1)} %tok_ref.1) | copy-start | bytes 1769476
  4.2 1.1 %copy-start.3 = (bf16[128,2304]{1,0:T(8,128)(2,1)S(1)}, bf16[128,2304]{1,0:T(8,128)(2,1)}, u32[]{:S(2)}) copy-start(bf16[128,2304]{1,0:T(8,128)(2,1)} %cot_ref.1) | copy-start | bytes 1769476
  91.6 2.3 %copy-start = (bf16[2,512,2304]{2,1,0:T(8,128)(2,1)S(1)}, bf16[2,512,2304]{2,1,0:T(8,128)(2,1)}, u32[]{:S(2)}) copy-start(bf16[2,512,2304]{2,1,0:T(8,128)(2,1)} %get-tuple-element.9.x_ref) | copy-start | bytes 14155780

commit v4 on v3

--- a/solution.py
+++ b/solution.py
@@ -47,7 +47,7 @@
 def main_kernel(n_wide, n_node, chunks,
                 ids_ref, tok_ref, cot_ref, tiles_ref,
                 mixed_ref, input_ref, gath_ref, acts_ref,
-                blocks, all_ids, ids_now, inv_vec, inv_ref, weights, acts, parts, arrived,
+                blocks, all_ids, ids_now, inv_vec, inv_ref, tok_now, cot_now, weights, acts, parts, arrived,
                 zsend, zrecv, ysend, yrecv, isend, irecv, lsem,
                 xsend, xrecv, nsend, nrecv, hsend, hrecv, psend, precv, osend, orecv, ssem):
     w = lax.axis_index("wide")
@@ -82,8 +82,9 @@
     def keep(t):
         return pltpu.make_async_copy((tok_ref, cot_ref)[t], gath_ref.at[t, own_rows, :], ssem.at[t])
 
-    keep(0).start()
-    keep(1).start()
+    def load(t):
+        return pltpu.make_async_copy((tok_ref, cot_ref)[t], (tok_now, cot_now)[t], lsem.at[3 + t])
+
     pl.semaphore_wait(barrier, n_wide + n_node - 1)
 
     def both_ways(d, action):
@@ -205,6 +206,9 @@
         for k in range(chunks):
             both_ways(d, z_pass(k))
     both_ways(0, x_begin)
+    for t in range(2):
+        load(t).start()
+        keep(t).start()
 
     for d in range(1, n_wide):
         j = lax.rem(w + d, n_wide)
@@ -243,11 +247,13 @@
     lax.fori_loop(0, rblocks, place, 0)
     both_ways(1, x_pass)
 
-    gate = jnp.dot(tok_ref[...], weights[0], preferred_element_type=jnp.float32)
-    up = jnp.dot(tok_ref[...], weights[1], preferred_element_type=jnp.float32)
+    load(0).wait()
+    load(1).wait()
+    gate = jnp.dot(tok_now[...], weights[0], preferred_element_type=jnp.float32)
+    up = jnp.dot(tok_now[...], weights[1], preferred_element_type=jnp.float32)
     value, slope = gelu_parts(gate)
     hidden = (value * up).astype(jnp.bfloat16)
-    hidden_grad = jnp.dot(cot_ref[...], weights[2], preferred_element_type=jnp.float32)
+    hidden_grad = jnp.dot(cot_now[...], weights[2], preferred_element_type=jnp.float32)
     gate_grad = (hidden_grad * up * slope).astype(jnp.bfloat16)
     up_grad = (hidden_grad * value).astype(jnp.bfloat16)
     acts[0] = gate_grad
@@ -381,7 +387,7 @@
             jax.ShapeDtypeStruct((2, n_wide * toks, width), bf16),
             jax.ShapeDtypeStruct((3, n_wide * toks, FF_DEV), bf16),
         ),
-        in_specs=[vmem, vmem, vmem, vmem],
+        in_specs=[vmem, hbm, hbm, hbm],
         out_specs=(vmem, vmem, hbm, hbm),
         scratch_shapes=[
             pltpu.VMEM((n_wide * slots + 1, EDGE, EDGE), bf16),
@@ -389,18 +395,20 @@
             pltpu.SMEM((n_wide, 8, EDGE), jnp.int32),
             pltpu.VMEM((8, EDGE), jnp.int32),
             pltpu.SMEM((8, EDGE), jnp.int32),
+            pltpu.VMEM((toks, width), bf16),
+            pltpu.VMEM((toks, width), bf16),
             pltpu.VMEM((3, width, FF_DEV), bf16),
             pltpu.VMEM((3, toks, FF_DEV), bf16),
             pltpu.VMEM((2, toks, width), bf16),
             pltpu.VMEM((2, n_node, toks // n_node, width), bf16),
             dma((2, n_wide, chunks)), dma((n_wide, chunks)), dma((n_wide, chunks)), dma((n_wide, chunks)),
-            dma((n_wide,)), dma((n_wide,)), dma((3,)),
+            dma((n_wide,)), dma((n_wide,)), dma((5,)),
             dma((2, n_wide, 2)), dma((n_wide, 2)), dma((n_wide, n_node)), dma((n_wide, n_node)),
             dma((2, n_wide)), dma((n_wide,)), dma((2, n_node)), dma((2, n_node)), dma((2, n_node)), dma((2, n_node)),
             dma((3,)),
         ],
         compiler_params=pltpu.CompilerParams(
-            collective_id=1, has_side_effects=True, vmem_limit_bytes=48 << 20
+            collective_id=1, has_side_effects=True, vmem_limit_bytes=60 << 20
         ),
     )(ids, tokens, cotangent, tiles)
 
@@ -442,7 +450,7 @@
             out_specs=pl.BlockSpec((slots, EDGE, EDGE), lambda j, ids: (0, 0, 0)),
             scratch_shapes=[pltpu.VMEM((slots, EDGE, EDGE), jnp.float32)],
         ),
-        compiler_params=pltpu.CompilerParams(vmem_limit_bytes=24 << 20),
+        compiler_params=pltpu.CompilerParams(vmem_limit_bytes=60 << 20),
     )(mine, gathered, acts)
 
 

time: 101 us -> 99.5 us (0.985)
  local copies, waits for them, and re-layouts: 7.24 us -> 2.24 us
  Pallas kernels: 91.2 us -> 95.1 us
    unnamed x10 -> x8, local copies, waits for them, and re-layouts: 7.23 us -> 1.64 us
    pallas_call x1, Pallas kernels: 86.3 us -> 88.3 us  [main_call(): pl.pallas_call(functools.partial(main_kernel, n_wide, n_node, chunks), ou...]
    pallas_call x1, Pallas kernels: 4.89 us -> 6.78 us  [slot_grads(): pl.pallas_call(functools.partial(grads_kernel, slots, width // EDGE), out...]
where the time goes in v4:
time: 99.5 us; the launch traced here: 99.3 us
  Pallas kernels  95.1 us (96%)
  local copies, waits for them, and re-layouts  2.24 us (2%)
  between operations  1.31 us (1%)
    pallas_call x1, Pallas kernels, main_call(): pl.pallas_call(functools.partial(main_kernel, n_wide, n_node, chunks), ou...  88.3 us
    pallas_call x1, Pallas kernels, slot_grads(): pl.pallas_call(functools.partial(grads_kernel, slots, width // EDGE), out...  6.78 us

profile of v4, /device:TPU:1, one launch (start us, length us, event | category | flops | bytes accessed | tf_op | source)
XLA Modules:
  0.0 99.3 jit_solution(13859193844214372586)
XLA Ops:
  1.3 0.7 compare_select_fusion.mine_ref
  1.9 0.0 copy-start.2
  1.9 0.6 broadcast_in_dim.14.ids_ref
  2.5 88.3 %shard_map.76 = (bf16[128,2304]{1,0:T(8,128)(2,1)}, bf16[128,2304]{1,0:T(8,128)(2,1)}, bf16[2,512,2304]{2,1,0:T(8,128)(2,1)}, bf16[3,512,512]{2,1,0:T(8,128)(2,1)}) custom-call(s32[8,128]{1,0:T(8,128)} %broadcast_in_dim.14.ids_ref, bf16[128,2304]{1,0:T(8,128)(2,1)} %tok_ref.1, bf16[128,2304]{1,0:T(8,128)(2,1)} %cot_ref.1, bf16[25,128,128]{2,1,0:T(8,128)(2,1)} %bitcast.7), custom_call_target="tpu_custom_call" | custom-call | tf_op jit(solution)/shard_map/pallas_call | solution.py:382
  90.9 0.0 copy-start.1
  90.9 0.0 copy-start
  90.9 0.0 copy-done.2
  90.9 6.8 %shard_map.77 = bf16[25,128,128]{2,1,0:T(8,128)(2,1)} custom-call(s32[25]{0:T(128)} %copy-done.2, bf16[2,512,2304]{2,1,0:T(8,128)(2,1)} %get-tuple-element.9.x_ref, bf16[3,512,512]{2,1,0:T(8,128)(2,1)} %get-tuple-element.10.acts_ref), custom_call_target="tpu_custom_call" | custom-call | tf_op jit(solution)/shard_map/pallas_call | solution.py:440
  97.7 0.0 copy-done.1
  97.7 0.8 copy.11
  98.5 0.0 copy-done
  98.5 0.8 copy.12
  (1 shorter events, 0.0 us)
Async XLA Ops:
  1.9 89.0 %copy-start.2 = (s32[25]{0:T(128)}, s32[25]{0:T(128)S(1)}, u32[]{:S(2)}) copy-start(s32[25]{0:T(128)S(1)} %compare_select_fusion.mine_ref) | copy-start | bytes 304
  90.9 6.8 %copy-start.1 = (bf16[128,2304]{1,0:T(8,128)(2,1)S(1)}, bf16[128,2304]{1,0:T(8,128)(2,1)}, u32[]{:S(2)}) copy-start(bf16[128,2304]{1,0:T(8,128)(2,1)} %get-tuple-element.14) | copy-start | bytes 1769476
  90.9 7.6 %copy-start = (bf16[128,2304]{1,0:T(8,128)(2,1)S(1)}, bf16[128,2304]{1,0:T(8,128)(2,1)}, u32[]{:S(2)}) copy-start(bf16[128,2304]{1,0:T(8,128)(2,1)} %get-tuple-element.15) | copy-start | bytes 1769476

commit v5 on v4

--- a/solution.py
+++ b/solution.py
@@ -307,9 +307,9 @@
 
     out_refs = (mixed_ref, input_ref)
 
-    def o_copy(t, src, to, d):
-        at = out_refs[t].at[pl.ds(pl.multiple_of(src * piece, 16), piece), :]
-        return remote(at, at, osend.at[t, d], orecv.at[t, src], {"node": to})
+    def o_copy(t, q, b, slot):
+        at = out_refs[t].at[pl.ds(pl.multiple_of(q * piece, 16), piece), :]
+        return remote(at, at, osend.at[t, slot], orecv.at[t, q], {"node": flip(b)})
 
     def reduce_part(t):
         mine = pl.ds(pl.multiple_of(n * piece, 16), piece)
@@ -319,15 +319,25 @@
             p_copy(t, src, src, d).wait_recv()
             acc = acc + arrived[t, src].astype(jnp.float32)
         out_refs[t][mine, :] = acc.astype(jnp.bfloat16)
-        for d in range(1, n_node):
-            o_copy(t, n, lax.rem(n + d, n_node), d).start()
+        o_copy(t, n, bits - 1, 0).start()
 
     both_ways(1, h_pass)
-    reduce_part(0)
     for d in range(3, n_wide):
         both_ways(d, x_pass)
         both_ways(d - 1, h_pass)
+    reduce_part(0)
     reduce_part(1)
+    for t in range(2):
+        slot = 1
+        for b in reversed(range(bits - 1)):
+            held = held_at(b)
+            for q in held:
+                @pl.when(lax.rem(q // (1 << (b + 1)), 2) != lax.rem(n // (1 << (b + 1)), 2))
+                def _():
+                    o_copy(t, q, b, slot).wait_recv()
+            for q in held:
+                o_copy(t, q, b, slot).start()
+                slot += 1
     for d in range(1, n_wide):
         j = lax.rem(w + d, n_wide)
         slot = 1
@@ -350,9 +360,14 @@
     for t in range(2):
         for d in range(1, n_node):
             src = lax.rem(n + d, n_node)
-            o_copy(t, src, src, d).wait_recv()
-            o_copy(t, n, src, d).wait_send()
             p_copy(t, n, src, d).wait_send()
+        for i in last:
+            o_copy(t, i + (1 - n % 2), 0, 0).wait_recv()
+        slot = 0
+        for b in reversed(range(bits)):
+            for q in held_at(b):
+                o_copy(t, q, b, slot).wait_send()
+                slot += 1
     for d in range(1, n_wide):
         hops(lambda j, q, b, slot: n_copy(j, q, b, slot).wait_send(), d)
 

time: 99.5 us -> 97.9 us (0.984)
  Pallas kernels: 95.1 us -> 93.4 us
    pallas_call x1, Pallas kernels: 88.3 us -> 86.7 us  [main_call(): pl.pallas_call(functools.partial(main_kernel, n_wide, n_node, chunks), ou...]
where the time goes in v5:
time: 97.9 us; the launch traced here: 97.6 us
  Pallas kernels  93.4 us (95%)
  local copies, waits for them, and re-layouts  2.24 us (2%)
  between operations  1.31 us (1%)
    pallas_call x1, Pallas kernels, main_call(): pl.pallas_call(functools.partial(main_kernel, n_wide, n_node, chunks), ou...  86.7 us
    pallas_call x1, Pallas kernels, slot_grads(): pl.pallas_call(functools.partial(grads_kernel, slots, width // EDGE), out...  6.78 us

profile of v5, /device:TPU:1, one launch (start us, length us, event | category | flops | bytes accessed | tf_op | source)
XLA Modules:
  0.0 97.6 jit_solution(5000432893587555582)
XLA Ops:
  1.3 0.7 compare_select_fusion.mine_ref
  1.9 0.0 copy-start.2
  1.9 0.6 broadcast_in_dim.14.ids_ref
  2.5 86.7 %shard_map.76 = (bf16[128,2304]{1,0:T(8,128)(2,1)}, bf16[128,2304]{1,0:T(8,128)(2,1)}, bf16[2,512,2304]{2,1,0:T(8,128)(2,1)}, bf16[3,512,512]{2,1,0:T(8,128)(2,1)}) custom-call(s32[8,128]{1,0:T(8,128)} %broadcast_in_dim.14.ids_ref, bf16[128,2304]{1,0:T(8,128)(2,1)} %tok_ref.1, bf16[128,2304]{1,0:T(8,128)(2,1)} %cot_ref.1, bf16[25,128,128]{2,1,0:T(8,128)(2,1)} %bitcast.7), custom_call_target="tpu_custom_call" | custom-call | tf_op jit(solution)/shard_map/pallas_call | solution.py:397
  89.2 0.0 copy-start.1
  89.2 0.0 copy-start
  89.2 0.0 copy-done.2
  89.2 6.8 %shard_map.77 = bf16[25,128,128]{2,1,0:T(8,128)(2,1)} custom-call(s32[25]{0:T(128)} %copy-done.2, bf16[2,512,2304]{2,1,0:T(8,128)(2,1)} %get-tuple-element.9.x_ref, bf16[3,512,512]{2,1,0:T(8,128)(2,1)} %get-tuple-element.10.acts_ref), custom_call_target="tpu_custom_call" | custom-call | tf_op jit(solution)/shard_map/pallas_call | solution.py:455
  96.0 0.0 copy-done.1
  96.0 0.8 copy.11
  96.8 0.0 copy-done
  96.8 0.8 copy.12
  (1 shorter events, 0.0 us)
Async XLA Ops:
  1.9 87.3 %copy-start.2 = (s32[25]{0:T(128)}, s32[25]{0:T(128)S(1)}, u32[]{:S(2)}) copy-start(s32[25]{0:T(128)S(1)} %compare_select_fusion.mine_ref) | copy-start | bytes 304
  89.2 6.8 %copy-start.1 = (bf16[128,2304]{1,0:T(8,128)(2,1)S(1)}, bf16[128,2304]{1,0:T(8,128)(2,1)}, u32[]{:S(2)}) copy-start(bf16[128,2304]{1,0:T(8,128)(2,1)} %get-tuple-element.14) | copy-start | bytes 1769476
  89.2 7.6 %copy-start = (bf16[128,2304]{1,0:T(8,128)(2,1)S(1)}, bf16[128,2304]{1,0:T(8,128)(2,1)}, u32[]{:S(2)}) copy-start(bf16[128,2304]{1,0:T(8,128)(2,1)} %get-tuple-element.15) | copy-start | bytes 1769476
